TPU v7x, 512 devices: a whole 4x4x16 slice. The times are simulated.
512 devices in a mesh: rx: 32 (over z_lo, x), tx: 16 (over y, z_hi, core).
Axes of the slice: x: 4, y: 4, z: 16 (z_hi: 2, z_lo: 8; z = z_hi * 8 + z_lo), core: 2. Of those that a mesh axis runs over, the one named last changes fastest.
Arguments:
- sender_xy: int32 [2, 32768], P(None, ('tx', 'rx')), may hold values from 0 to 255, as said below
- listener_xy: int32 [2, 32768], P(None, ('rx', 'tx')), may hold values from 0 to 256, as said below
- powers: float32 [32768, 128], P(('tx', 'rx')), may hold values from 0.25 to 1
- weight: int32 [32768], P(('rx', 'tx')), may hold values from 1 to 16
- fairness: int32 [32768], P(('rx', 'tx')), may hold values from 0 to 2
- step_code: int32 [1], replicated, may hold values from 256 to 4096
Outputs:
- quality: float32 [32768, 128], P(('rx', 'tx'))
- gradient: float32 [32768, 128], P(('tx', 'rx'))
- new_power: float32 [32768, 128], P(('tx', 'rx'))
- duality_gap: float32 [1], replicated
Inputs may be any that keep to these rules, and one draw needn't show every extreme that they name: `sender_xy`: row 0 lies in 0 to 255 and row 1 in 0 to 255. `listener_xy`: each entry equals the sender_xy entry of the same user or exceeds it by one.
All inputs are finite; a program needn't handle non-finite values.
Results may differ from a plain program's by a relative error of at most 0.0003.
Values sent between devices are 32-bit elements; how exact they have to be, the bound alone decides.
No kernel may reach another device: no remote copies, remote signals or barrier semaphores. Data moves between devices by JAX's collectives and lax.ppermute only.
A program may use at most 64 MiB of HBM per device.

v0:
```python
import jax
import jax.numpy as jnp
from jax import lax
from jax.sharding import PartitionSpec as P

NOISE_POWER = 0.05
ARRAY_GAIN = 32.0
WEIGHT_UNIT = 1.0 / 16.0
PEAK_POWER = 1.0


def path_gain(listen, sender):
    delta_x = listen[0].astype(jnp.float32)[:, None] - sender[0].astype(jnp.float32)[None, :]
    delta_y = listen[1].astype(jnp.float32)[:, None] - sender[1].astype(jnp.float32)[None, :]
    return 1.0 / (1.0 + delta_x * delta_x + delta_y * delta_y)


def derivatives(interference, signal, user_weight, user_fair):
    denominator = NOISE_POWER + interference
    quality = signal / denominator
    user_scale = WEIGHT_UNIT * user_weight.astype(jnp.float32)
    marginal = (
        user_scale[:, None]
        * jnp.exp(-user_fair.astype(jnp.float32)[:, None] * jnp.log(quality))
        / denominator
    )
    return (quality, marginal, marginal * quality)


def per_device(sender_xy, listener_xy, powers, weight, fairness, step_code):
    rx_here = lax.axis_index("rx")
    tx_here = lax.axis_index("tx")
    user_rows = powers.shape[0]
    channels = powers.shape[1]
    senders, sender_power = (
        lax.all_gather(sender_xy, "rx", axis=1, tiled=True),
        lax.all_gather(powers, "rx", axis=0, tiled=True),
    )
    listeners = lax.all_gather(listener_xy, "tx", axis=1, tiled=True)
    rx_width = listeners.shape[1]
    tx_width = senders.shape[1]
    row_start = rx_here * rx_width
    col_start = tx_here * tx_width
    gain_tile = path_gain(listeners, senders)
    row_ids = row_start + jnp.arange(rx_width, dtype=jnp.int32)
    col_ids = col_start + jnp.arange(tx_width, dtype=jnp.int32)
    diagonal = row_ids[:, None] == col_ids[None, :]
    crossing = jnp.where(diagonal, 0.0, gain_tile)
    own_gain = jnp.sum(jnp.where(diagonal, gain_tile, 0.0), axis=1)
    offset = row_start % tx_width
    interference_part = jnp.dot(crossing, sender_power, precision=lax.Precision.HIGHEST)
    signal_part = (
        ARRAY_GAIN * own_gain[:, None] * lax.dynamic_slice_in_dim(sender_power, offset, rx_width, 0)
    )
    interference, signal = (
        lax.psum_scatter(interference_part, "tx", scatter_dimension=0, tiled=True),
        lax.psum_scatter(signal_part, "tx", scatter_dimension=0, tiled=True),
    )
    quality, marginal, pressure = derivatives(interference, signal, weight, fairness)
    marginal_all, pressure_all = (
        lax.all_gather(marginal, "tx", axis=0, tiled=True),
        lax.all_gather(pressure, "tx", axis=0, tiled=True),
    )
    own_term = ARRAY_GAIN * own_gain[:, None] * marginal_all
    own_full = lax.dynamic_update_slice_in_dim(
        jnp.zeros((tx_width, channels), jnp.float32), own_term, offset, 0
    )
    pushed = lax.dot_general(
        crossing, pressure_all, (((0,), (0,)), ((), ())), precision=lax.Precision.HIGHEST
    )
    totals = lax.psum(own_full - pushed, "rx")
    gradient = lax.dynamic_slice_in_dim(totals, rx_here * user_rows, user_rows, 0)
    target = PEAK_POWER * jax.nn.sigmoid(gradient)
    step_size = step_code[0].astype(jnp.float32) / 4096.0
    new_power = powers + step_size * (target - powers)
    gap_local = jnp.sum(PEAK_POWER * jnp.maximum(gradient, 0.0) - gradient * powers)
    gap_sum = lax.psum(gap_local, ("rx", "tx"))
    duality_gap = (
        gap_sum / (user_rows * channels * lax.axis_size("rx") * lax.axis_size("tx"))
    ).reshape(1)
    return (quality, gradient, new_power, duality_gap)


def solution(mesh):
    placed = (
        P(None, ("tx", "rx")),
        P(None, ("rx", "tx")),
        P(("tx", "rx"), None),
        P(("rx", "tx")),
        P(("rx", "tx")),
        P(),
    )
    return jax.shard_map(
        per_device,
        mesh=mesh,
        in_specs=placed,
        out_specs=(P(("rx", "tx"), None), P(("tx", "rx"), None), P(("tx", "rx"), None), P()),
        check_vma=False,
    )
```

profile of v0, /device:TPU:1, one launch (start us, length us, event | category | flops | bytes accessed | tf_op | source)
XLA Modules:
  0.0 1118.0 jit_solution(16016938262697707755)
XLA Ops:
  7.2 0.0 all-gather.4.cloned.1.call-start
  7.2 0.7 all-gather.4.cloned.1.call-update
  7.9 0.0 reduce-scatter.3.cloned.1.call-start
  8.0 51.2 %all-gather = s32[16,64,2]{1,2,0:T(2,128)S(1)} all-gather(s32[1,64,2]{1,2,0:T(2,128)} %bitcast.34), channel_id=1, replica_groups=mesh['rx'=32,'tx'=16] {'tx'}, dimensions={0}, use_global_device_ids=true | all-gather | bytes 8704 | tf_op jit(solution)/shard_map/all_gather | solution.py:39
  59.1 0.1 reshape.43
  59.3 104.0 %all-gather.1 = s32[32,64,2]{1,2,0:T(2,128)S(1)} all-gather(s32[1,64,2]{1,2,0:T(2,128)} %bitcast.35), channel_id=1, replica_groups=mesh['rx'=32,'tx'=16] {'rx'}, dimensions={0}, use_global_device_ids=true | all-gather | bytes 16896 | tf_op jit(solution)/shard_map/all_gather | solution.py:36
  163.3 0.1 reshape.45
  163.5 3.1 fusion
  166.5 49.7 %all-gather.4.cloned.1.call-done = f32[2048,128]{1,0:T(8,128)} async-done(((f32[64,128]{1,0:T(8,128)}), f32[2048,128]{1,0:T(8,128)}) %all-gather.4.cloned.1.call-update) | async-done | bytes 1048592 | tf_op jit(solution)/shard_map/all_gather | solution.py:37
  216.2 0.0 copy-start.1
  216.2 2.1 dynamic-slice_multiply_fusion
  218.4 0.0 reduce-scatter.3.cloned.1.call-update
  218.4 0.0 copy-start.3
  218.4 0.0 copy-start.4
  218.4 0.0 reduce-scatter.5.cloned.1.call-start
  218.5 0.0 copy-done.1
  218.5 9.3 fusion.2
  227.8 0.0 reduce-scatter.5.cloned.1.call-update
  227.8 0.0 all-reduce.2.cloned.1.call-start
  227.9 0.0 copy-done.3
  227.9 0.0 copy-done.4
  227.9 111.3 %reduce-scatter.3.cloned.1.call-done = f32[64,128]{1,0:T(8,128)} async-done(((f32[1024,128]{1,0:T(8,128)}), f32[64,128]{1,0:T(8,128)}) %reduce-scatter.3.cloned.1.call-update) | async-done | bytes 32784 | tf_op jit(solution)/shard_map/reduce_scatter | solution.py:57
  339.2 96.6 %reduce-scatter.5.cloned.1.call-done = f32[64,128]{1,0:T(8,128)} async-done(((f32[1024,128]{1,0:T(8,128)}), f32[64,128]{1,0:T(8,128)}) %reduce-scatter.5.cloned.1.call-update) | async-done | bytes 32784 | tf_op jit(solution)/shard_map/reduce_scatter | solution.py:56
  435.8 1.4 fusion.14
  437.2 43.2 %all_gather.18 = f32[1024,128]{1,0:T(8,128)S(1)} all-gather(f32[64,128]{1,0:T(8,128)S(1)} %get-tuple-element.7), channel_id=1, replica_groups=mesh['rx'=32,'tx'=16] {'tx'}, dimensions={0}, use_global_device_ids=true | all-gather | bytes 557056 | tf_op jit(solution)/shard_map/all_gather | solution.py:61
  480.4 49.4 %all_gather.19 = f32[1024,128]{1,0:T(8,128)S(1)} all-gather(f32[64,128]{1,0:T(8,128)S(1)} %get-tuple-element.6), channel_id=1, replica_groups=mesh['rx'=32,'tx'=16] {'tx'}, dimensions={0}, use_global_device_ids=true | all-gather | bytes 557056 | tf_op jit(solution)/shard_map/all_gather | solution.py:62
  529.7 0.1 broadcast_in_dim.7
  529.8 0.2 multiply_dynamic-update-slice_fusion
  530.0 16.3 %fusion.9 = f32[2048,128]{1,0:T(8,128)} fusion(f32[2048,128]{1,0:T(8,128)S(1)} %multiply_dynamic-update-slice_fusion, f32[1024,128]{1,0:T(8,128)S(1)} %all_gather.19, f32[2048]{0:T(1024)S(1)} %bitcast.27, f32[1024]{0:T(1024)S(1)} %bitcast.33, f32[2048]{0:T(1024)S(1)} %bitcast.24, f32[1024]{0:T(1024)S(1)} %bitcast.30, s32[2048]{0:T(1024)S(1)} %iota_add_fusion, ...), kind=kOutput, calls=%fused_computation.12 | convolution fusion | flops 3240361984 | bytes 2658304 | tf_op jit(solution)/shard_map/dot_general | solution.py:68
  546.3 0.0 copy-start
  546.3 0.0 all-reduce.2.cloned.1.call-update
  547.0 437.2 %all-reduce.2.cloned.1.call-done = f32[2048,128]{1,0:T(8,128)} async-done(((f32[2048,128]{1,0:T(8,128)}), f32[2048,128]{1,0:T(8,128)}) %all-reduce.2.cloned.1.call-update) | async-done | bytes 1048592 | tf_op jit(solution)/shard_map/psum | solution.py:71
  984.1 0.0 copy-done
  984.1 1.4 subtract_reduce_fusion
  985.5 0.0 copy-start.2
  985.5 123.6 %psum.15 = f32[]{:T(128)} all-reduce(f32[]{:T(128)} %get-tuple-element.4), channel_id=1, replica_groups=mesh['rx'=32,'tx'=16] {'rx','tx'}, use_global_device_ids=true, to_apply=%region_5.6 | all-reduce | flops 1 | bytes 8 | tf_op jit(solution)/shard_map/psum | solution.py:77
  1109.1 0.6 multiply_add_fusion
  1110.4 0.0 copy-done.2
  (8 shorter events, 0.0 us)
Async XLA Ops:
  7.2 209.1 %all-gather.4.cloned.1.call-start = ((), (), s32[]{:S(2)}) async-start(), calls=%async_computation.2 | async-start | bytes 1081344 | tf_op jit(solution)/shard_map/all_gather | solution.py:37
  7.9 331.3 %reduce-scatter.3.cloned.1.call-start = ((), (), s32[]{:S(2)}) async-start(), calls=%async_computation.3 | async-start | bytes 557056 | tf_op jit(solution)/shard_map/reduce_scatter | solution.py:57
  216.2 2.2 copy-start.1
  218.4 9.5 copy-start.3
  218.4 9.5 copy-start.4
  218.4 217.4 %reduce-scatter.5.cloned.1.call-start = ((), (), s32[]{:S(2)}) async-start(), calls=%async_computation.4 | async-start | bytes 557056 | tf_op jit(solution)/shard_map/reduce_scatter | solution.py:56
  227.8 756.3 %all-reduce.2.cloned.1.call-start = ((), (), s32[]{:S(2)}) async-start(), calls=%async_computation.5 | async-start | bytes 2097152 | tf_op jit(solution)/shard_map/psum | solution.py:71
  546.3 437.8 %copy-start = (f32[64,128]{1,0:T(8,128)S(1)}, f32[64,128]{1,0:T(8,128)}, u32[]{:S(2)}) copy-start(f32[64,128]{1,0:T(8,128)} %param.8) | copy-start | bytes 98308
  985.5 124.9 %copy-start.2 = (f32[64,128]{1,0:T(8,128)}, f32[64,128]{1,0:T(8,128)S(1)}, u32[]{:S(2)}) copy-start(f32[64,128]{1,0:T(8,128)S(1)} %get-tuple-element.5) | copy-start | bytes 98308
Sparse Core Ops, SparseCore 0:
  10.1 206.1 all-gather.3
  220.9 118.3 reduce-scatter.2
  344.6 91.1 reduce-scatter.4
  546.4 437.6 all-reduce.1
where the time goes:
time: 1120 us
  waiting for transfers between devices  695 us (62%)
  blocking collectives  371 us (33%)
  matrix products  25.6 us (2%)
  between operations  16.3 us (1%)
    psum x1, waiting for transfers between devices, per_device(): totals = lax.psum(own_full - pushed, 'rx')  437 us
    psum x1, blocking collectives, per_device(): gap_sum = lax.psum(gap_local, ('rx', 'tx'))  124 us
    reduce_scatter x1, waiting for transfers between devices, per_device(): lax.psum_scatter(signal_part, 'tx', scatter_dimension=0, tiled=True)  111 us
    all_gather x1, blocking collectives, per_device(): lax.all_gather(sender_xy, 'rx', axis=1, tiled=True)  104 us
    reduce_scatter x1, waiting for transfers between devices, per_device(): lax.psum_scatter(interference_part, 'tx', scatter_dimension=0, tiled=True)  96.6 us
    all_gather x1, blocking collectives, per_device(): listeners = lax.all_gather(listener_xy, 'tx', axis=1, tiled=True)  51.2 us
    all_gather x1, waiting for transfers between devices, per_device(): lax.all_gather(powers, 'rx', axis=0, tiled=True)  49.7 us
    all_gather x1, blocking collectives, per_device(): lax.all_gather(pressure, 'tx', axis=0, tiled=True)  49.4 us
  transfers between devices with their start and end apart: 4, of which 4 were waited for; matrix products, arithmetic and copies ran while one was open for 1% of the time, Pallas kernels for 0%

commit v1 on v0

--- a/solution.py
+++ b/solution.py
@@ -2,6 +2,7 @@
 import jax.numpy as jnp
 from jax import lax
 from jax.sharding import PartitionSpec as P
+from jax.lax import all_to_all, psum
 
 NOISE_POWER = 0.05
 ARRAY_GAIN = 32.0
@@ -59,7 +60,9 @@
     quality, marginal, pressure = derivatives(interference, signal, weight, fairness)
     marginal_all, pressure_all = (
         lax.all_gather(marginal, "tx", axis=0, tiled=True),
-        lax.all_gather(pressure, "tx", axis=0, tiled=True),
+        jnp.concatenate(
+            all_to_all(jnp.stack([pressure for _ in range(psum(1, "tx"))], 0), "tx", 0, 0), 0
+        ),
     )
     own_term = ARRAY_GAIN * own_gain[:, None] * marginal_all
     own_full = lax.dynamic_update_slice_in_dim(

time: 1120 us -> 1100 us (0.982)
  blocking collectives: 371 us -> 342 us
    all_gather x1 -> x0, blocking collectives: 49.4 us -> none  [per_device(): lax.all_gather(pressure, 'tx', axis=0, tiled=True)]
    all_gather x1, blocking collectives: 43.2 us -> 63 us  [per_device(): lax.all_gather(marginal, 'tx', axis=0, tiled=True)]
  transfers between devices with their start and end apart: 4 -> 5, of which waited for: 4 -> 4; matrix products, arithmetic and copies ran while one was open for 1% -> 1% of each run, Pallas kernels for 0% -> 0%
where the time goes in v1:
time: 1100 us
  waiting for transfers between devices  699 us (64%)
  blocking collectives  342 us (31%)
  matrix products  25.6 us (2%)
  between operations  16.3 us (1%)
    psum x1, waiting for transfers between devices, per_device(): totals = lax.psum(own_full - pushed, 'rx')  440 us
    psum x1, blocking collectives, per_device(): gap_sum = lax.psum(gap_local, ('rx', 'tx'))  124 us
    reduce_scatter x1, waiting for transfers between devices, per_device(): lax.psum_scatter(signal_part, 'tx', scatter_dimension=0, tiled=True)  111 us
    all_gather x1, blocking collectives, per_device(): lax.all_gather(sender_xy, 'rx', axis=1, tiled=True)  104 us
    reduce_scatter x1, waiting for transfers between devices, per_device(): lax.psum_scatter(interference_part, 'tx', scatter_dimension=0, tiled=True)  96.6 us
    all_gather x1, blocking collectives, per_device(): lax.all_gather(marginal, 'tx', axis=0, tiled=True)  63 us
    all_gather x1, blocking collectives, per_device(): listeners = lax.all_gather(listener_xy, 'tx', axis=1, tiled=True)  51.2 us
    all_gather x1, waiting for transfers between devices, per_device(): lax.all_gather(powers, 'rx', axis=0, tiled=True)  49.7 us
  transfers between devices with their start and end apart: 5, of which 4 were waited for; matrix products, arithmetic and copies ran while one was open for 1% of the time, Pallas kernels for 0%

profile of v1, /device:TPU:1, one launch (start us, length us, event | category | flops | bytes accessed | tf_op | source)
XLA Modules:
  0.0 1098.6 jit_solution(9321447099170479233)
XLA Ops:
  7.2 0.0 all-gather.4.cloned.1.call-start
  7.2 0.7 all-gather.4.cloned.1.call-update
  7.9 0.0 reduce-scatter.3.cloned.1.call-start
  8.0 51.2 %all-gather = s32[16,64,2]{1,2,0:T(2,128)S(1)} all-gather(s32[1,64,2]{1,2,0:T(2,128)} %bitcast.36), channel_id=1, replica_groups=mesh['rx'=32,'tx'=16] {'tx'}, dimensions={0}, use_global_device_ids=true | all-gather | bytes 8704 | tf_op jit(solution)/shard_map/all_gather | solution.py:40
  59.1 0.1 reshape.49
  59.3 104.0 %all-gather.1 = s32[32,64,2]{1,2,0:T(2,128)S(1)} all-gather(s32[1,64,2]{1,2,0:T(2,128)} %bitcast.37), channel_id=1, replica_groups=mesh['rx'=32,'tx'=16] {'rx'}, dimensions={0}, use_global_device_ids=true | all-gather | bytes 16896 | tf_op jit(solution)/shard_map/all_gather | solution.py:37
  163.3 0.1 reshape.51
  163.5 3.1 fusion
  166.5 49.7 %all-gather.4.cloned.1.call-done = f32[2048,128]{1,0:T(8,128)} async-done(((f32[64,128]{1,0:T(8,128)}), f32[2048,128]{1,0:T(8,128)}) %all-gather.4.cloned.1.call-update) | async-done | bytes 1048592 | tf_op jit(solution)/shard_map/all_gather | solution.py:38
  216.2 0.0 copy-start.1
  216.2 2.1 dynamic-slice_multiply_fusion
  218.4 0.0 reduce-scatter.3.cloned.1.call-update
  218.4 0.0 copy-start.3
  218.4 0.0 copy-start.4
  218.4 0.0 reduce-scatter.5.cloned.1.call-start
  218.5 0.0 copy-done.1
  218.5 9.3 fusion.2
  227.8 0.0 reduce-scatter.5.cloned.1.call-update
  227.8 0.0 copy-done.3
  227.8 0.0 copy-done.4
  227.8 111.4 %reduce-scatter.3.cloned.1.call-done = f32[64,128]{1,0:T(8,128)} async-done(((f32[1024,128]{1,0:T(8,128)}), f32[64,128]{1,0:T(8,128)}) %reduce-scatter.3.cloned.1.call-update) | async-done | bytes 32784 | tf_op jit(solution)/shard_map/reduce_scatter | solution.py:58
  339.2 96.6 %reduce-scatter.5.cloned.1.call-done = f32[64,128]{1,0:T(8,128)} async-done(((f32[1024,128]{1,0:T(8,128)}), f32[64,128]{1,0:T(8,128)}) %reduce-scatter.5.cloned.1.call-update) | async-done | bytes 32784 | tf_op jit(solution)/shard_map/reduce_scatter | solution.py:57
  435.8 1.4 fusion.14
  437.2 0.8 stack.2
  438.0 6.0 all-to-all-start
  444.0 0.0 all-reduce.2.cloned.1.call-start
  444.1 63.0 %all_gather.15 = f32[1024,128]{1,0:T(8,128)S(1)} all-gather(f32[64,128]{1,0:T(8,128)S(1)} %get-tuple-element.7), channel_id=1, replica_groups=mesh['rx'=32,'tx'=16] {'tx'}, dimensions={0}, use_global_device_ids=true | all-gather | bytes 557056 | tf_op jit(solution)/shard_map/all_gather | solution.py:62
  507.1 0.1 broadcast_in_dim.7
  507.2 0.2 multiply_dynamic-update-slice_fusion
  507.4 0.0 all-to-all-done
  507.4 16.3 %fusion.9 = f32[2048,128]{1,0:T(8,128)} fusion(f32[2048,128]{1,0:T(8,128)S(1)} %multiply_dynamic-update-slice_fusion, f32[1024,128]{1,0:T(8,128)S(1)} %bitcast.21, f32[2048]{0:T(1024)S(1)} %bitcast.29, f32[1024]{0:T(1024)S(1)} %bitcast.35, f32[2048]{0:T(1024)S(1)} %bitcast.26, f32[1024]{0:T(1024)S(1)} %bitcast.32, s32[2048]{0:T(1024)S(1)} %iota_add_fusion, ...), kind=kOutput, calls=%fused_computation.12 | convolution fusion | flops 3240361984 | bytes 2658304 | tf_op jit(solution)/shard_map/dot_general | solution.py:71
  523.7 0.0 copy-start
  523.7 0.0 all-reduce.2.cloned.1.call-update
  524.4 440.3 %all-reduce.2.cloned.1.call-done = f32[2048,128]{1,0:T(8,128)} async-done(((f32[2048,128]{1,0:T(8,128)}), f32[2048,128]{1,0:T(8,128)}) %all-reduce.2.cloned.1.call-update) | async-done | bytes 1048592 | tf_op jit(solution)/shard_map/psum | solution.py:74
  964.7 0.0 copy-done
  964.7 1.4 subtract_reduce_fusion
  966.0 0.0 copy-start.2
  966.0 123.6 %psum.15 = f32[]{:T(128)} all-reduce(f32[]{:T(128)} %get-tuple-element.4), channel_id=1, replica_groups=mesh['rx'=32,'tx'=16] {'rx','tx'}, use_global_device_ids=true, to_apply=%region_5.6 | all-reduce | flops 1 | bytes 8 | tf_op jit(solution)/shard_map/psum | solution.py:80
  1089.6 0.6 multiply_add_fusion
  1090.9 0.0 copy-done.2
  (8 shorter events, 0.0 us)
Async XLA Ops:
  7.2 209.1 %all-gather.4.cloned.1.call-start = ((), (), s32[]{:S(2)}) async-start(), calls=%async_computation.3 | async-start | bytes 1081344 | tf_op jit(solution)/shard_map/all_gather | solution.py:38
  7.9 331.3 %reduce-scatter.3.cloned.1.call-start = ((), (), s32[]{:S(2)}) async-start(), calls=%async_computation.4 | async-start | bytes 557056 | tf_op jit(solution)/shard_map/reduce_scatter | solution.py:58
  216.2 2.2 copy-start.1
  218.4 9.4 copy-start.3
  218.4 9.4 copy-start.4
  218.4 217.4 %reduce-scatter.5.cloned.1.call-start = ((), (), s32[]{:S(2)}) async-start(), calls=%async_computation.5 | async-start | bytes 557056 | tf_op jit(solution)/shard_map/reduce_scatter | solution.py:57
  438.0 69.4 %all-to-all-start = ((f32[16,64,128]{2,1,0:T(8,128)}), f32[16,64,128]{2,1,0:T(8,128)S(1)}, u32[]{:S(2)}, u32[]{:S(2)}) async-start(f32[16,64,128]{2,1,0:T(8,128)} %stack.2), calls=%async_computation.2 | async-start | bytes 1048576 | tf_op jit(solution)/shard_map/all_to_all | solution.py:64
  444.0 520.6 %all-reduce.2.cloned.1.call-start = ((), (), s32[]{:S(2)}) async-start(), calls=%async_computation.6 | async-start | bytes 2097152 | tf_op jit(solution)/shard_map/psum | solution.py:74
  523.7 441.0 %copy-start = (f32[64,128]{1,0:T(8,128)S(1)}, f32[64,128]{1,0:T(8,128)}, u32[]{:S(2)}) copy-start(f32[64,128]{1,0:T(8,128)} %param.8) | copy-start | bytes 98308
  966.0 124.9 %copy-start.2 = (f32[64,128]{1,0:T(8,128)}, f32[64,128]{1,0:T(8,128)S(1)}, u32[]{:S(2)}) copy-start(f32[64,128]{1,0:T(8,128)S(1)} %get-tuple-element.5) | copy-start | bytes 98308
Sparse Core Ops, SparseCore 0:
  10.1 206.1 all-gather.3
  220.9 118.3 reduce-scatter.2
  344.6 91.1 reduce-scatter.4
  523.8 440.7 all-reduce.1
